TPU v7x, 128 devices: a whole 4x4x4 slice. The times are simulated.
128 devices in a mesh: dp: 2 (over z_lo), ctx: 32 (over x, y, core), tensor: 2 (over z_hi).
Axes of the slice: x: 4, y: 4, z: 4 (z_hi: 2, z_lo: 2; z = z_hi * 2 + z_lo), core: 2. Of those that a mesh axis runs over, the one named last changes fastest.
Arguments:
- layer_input: bfloat16 [2, 4352, 384], P('dp', 'ctx'), may hold values from -6 to 6
- valid_count: int32 [2], P('dp'), may hold values from 4217 to 4352, as said below
- cotangent: bfloat16 [2, 4352, 384], P('dp', 'ctx'), may hold values from -6 to 6
- ln1_gain: bfloat16 [384], P('dp'), may hold values from 0.099609375 to 1.8984375
- ln1_bias: bfloat16 [384], P('dp'), may hold values from -3 to 3
- w_query: bfloat16 [384, 384], P('dp', 'tensor'), may hold values from -0.4375 to 0.4375
- b_query: bfloat16 [384], P(('tensor', 'dp')), may hold values from -3 to 3
- w_key: bfloat16 [384, 384], P('dp', 'tensor'), may hold values from -0.4375 to 0.4375
- w_value: bfloat16 [384, 384], P('dp', 'tensor'), may hold values from -0.3125 to 0.3125
- b_value: bfloat16 [384], P(('tensor', 'dp')), may hold values from -3 to 3
- w_out: bfloat16 [384, 384], P('tensor', 'dp'), may hold values from -2.5 to 2.5
- b_out: bfloat16 [384], P('dp'), may hold values from -3 to 3
- ln2_gain: bfloat16 [384], P('dp'), may hold values from 0.099609375 to 1.8984375
- ln2_bias: bfloat16 [384], P('dp'), may hold values from -3 to 3
- w_up: bfloat16 [384, 1536], P('dp', 'tensor'), may hold values from -0.3125 to 0.3125
- b_up: bfloat16 [1536], P(('tensor', 'dp')), may hold values from -3 to 3
- w_down: bfloat16 [1536, 384], P('tensor', 'dp'), may hold values from -0.15625 to 0.15625
- b_down: bfloat16 [384], P('dp'), may hold values from -3 to 3
Outputs:
- layer_output: bfloat16 [2, 4352, 384], P('dp', 'ctx')
- grad_input: float32 [2, 4352, 384], P('dp', 'ctx')
- grad_ln1_gain: float32 [384], P('dp')
- grad_ln1_bias: float32 [384], P('dp')
- grad_w_query: float32 [384, 384], P('dp', 'tensor')
- grad_b_query: float32 [384], P(('tensor', 'dp'))
- grad_w_key: float32 [384, 384], P('dp', 'tensor')
- grad_w_value: float32 [384, 384], P('dp', 'tensor')
- grad_b_value: float32 [384], P(('tensor', 'dp'))
- grad_w_out: float32 [384, 384], P('tensor', 'dp')
- grad_b_out: float32 [384], P('dp')
- grad_ln2_gain: float32 [384], P('dp')
- grad_ln2_bias: float32 [384], P('dp')
- grad_w_up: float32 [384, 1536], P('dp', 'tensor')
- grad_b_up: float32 [1536], P(('tensor', 'dp'))
- grad_w_down: float32 [1536, 384], P('tensor', 'dp')
- grad_b_down: float32 [384], P('dp')
Inputs may be any that keep to these rules, and one draw needn't show every extreme that they name: `valid_count`: every image has a valid token in the last 136 positions.
All inputs are finite; a program needn't handle non-finite values.
Results may differ from a plain program's by a relative error of at most 0.03.
Values may be sent and summed in bfloat16 or wider, within the bound.
A program may use at most 64 MiB of HBM per device.

v0:
```python
import jax
import jax.numpy as jnp
from jax import lax
from jax.sharding import PartitionSpec as P

HEAD = 64


EPSILON = 1e-06


def normalize(rows):
    center = rows - jnp.mean(rows, axis=-1, keepdims=True)
    spread = jnp.mean(center * center, axis=-1, keepdims=True)
    return center * lax.rsqrt(spread + EPSILON)


def layer_norm(rows, gain, shift):
    return normalize(rows) * gain + shift


def gelu_exact(values):
    return jax.nn.gelu(values, approximate=False)


def product(left, right):
    return jnp.dot(left, right, preferred_element_type=jnp.float32)


def masked_scores(query_heads, key_heads, key_mask, factor):
    scores = (
        jnp.einsum("qhe,khe->hqk", query_heads, key_heads, preferred_element_type=jnp.float32)
        * factor
    )
    return jnp.where(key_mask[None, None, :], scores, -1e30)


def on_device(
    layer_input,
    valid_count,
    cotangent,
    ln1_gain,
    ln1_bias,
    w_query,
    b_query,
    w_key,
    w_value,
    b_value,
    w_out,
    b_out,
    ln2_gain,
    ln2_bias,
    w_up,
    b_up,
    w_down,
    b_down,
):
    (
        gain1,
        shift1,
        wquery,
        bquery,
        wkey,
        wvalue,
        bvalue,
        wout,
        bout,
        gain2,
        shift2,
        wup,
        bup,
        wdown,
        bdown,
    ) = (
        lax.all_gather(ln1_gain, "dp", axis=0, tiled=True),
        lax.all_gather(ln1_bias, "dp", axis=0, tiled=True),
        lax.all_gather(w_query, "dp", axis=0, tiled=True),
        lax.all_gather(b_query, "dp", axis=0, tiled=True),
        lax.all_gather(w_key, "dp", axis=0, tiled=True),
        lax.all_gather(w_value, "dp", axis=0, tiled=True),
        lax.all_gather(b_value, "dp", axis=0, tiled=True),
        lax.all_gather(w_out, "dp", axis=1, tiled=True),
        lax.all_gather(b_out, "dp", axis=0, tiled=True),
        lax.all_gather(ln2_gain, "dp", axis=0, tiled=True),
        lax.all_gather(ln2_bias, "dp", axis=0, tiled=True),
        lax.all_gather(w_up, "dp", axis=0, tiled=True),
        lax.all_gather(b_up, "dp", axis=0, tiled=True),
        lax.all_gather(w_down, "dp", axis=1, tiled=True),
        lax.all_gather(b_down, "dp", axis=0, tiled=True),
    )
    tokens = layer_input[0].astype(jnp.float32)
    count = tokens.shape[0]
    half = wquery.shape[1]
    local_heads = half // HEAD
    seq_len = count * lax.axis_size("ctx")
    factor = HEAD ** (-0.5)
    limit = valid_count[0]
    own_pos = lax.axis_index("ctx") * count + jnp.arange(count)
    query_ok = own_pos < limit
    key_ok = jnp.arange(seq_len) < limit
    norm1, norm1_back = jax.vjp(
        layer_norm, tokens, gain1.astype(jnp.float32), shift1.astype(jnp.float32)
    )
    normed1 = norm1.astype(jnp.bfloat16)
    queries = (product(normed1, wquery) + bquery.astype(jnp.float32)).astype(jnp.bfloat16)
    keys_own = product(normed1, wkey).astype(jnp.bfloat16)
    values_own = (product(normed1, wvalue) + bvalue.astype(jnp.float32)).astype(jnp.bfloat16)
    whole = lax.all_gather(
        jnp.concatenate([keys_own, values_own], axis=1), "ctx", axis=0, tiled=True
    )
    keys_all = whole[:, :half].reshape(seq_len, local_heads, HEAD)
    values_all = whole[:, half:].reshape(seq_len, local_heads, HEAD)
    query_heads = queries.reshape(count, local_heads, HEAD)
    scores = masked_scores(query_heads, keys_all, key_ok, factor)
    peak = jnp.max(scores, axis=-1, keepdims=True)
    expo = jnp.exp(scores - peak)
    total = jnp.sum(expo, axis=-1, keepdims=True)
    probs = expo / total
    log_total = peak + jnp.log(total)
    attended = jnp.einsum(
        "hqk,khe->qhe", probs.astype(jnp.bfloat16), values_all, preferred_element_type=jnp.float32
    )
    attended_low = attended.reshape(count, half).astype(jnp.bfloat16)
    hidden1 = tokens + lax.psum(product(attended_low, wout), "tensor") + bout.astype(jnp.float32)
    norm2, norm2_back = jax.vjp(
        layer_norm, hidden1, gain2.astype(jnp.float32), shift2.astype(jnp.float32)
    )
    normed2 = norm2.astype(jnp.bfloat16)
    upper = product(normed2, wup) + bup.astype(jnp.float32)
    active, gelu_back = jax.vjp(gelu_exact, upper)
    active_low = active.astype(jnp.bfloat16)
    mixed = lax.psum(product(active_low, wdown).astype(jnp.bfloat16), "tensor").astype(jnp.float32)
    result = (hidden1 + mixed + bdown.astype(jnp.float32)).astype(jnp.bfloat16)[None]
    grad_out = cotangent[0].astype(jnp.float32) * query_ok[:, None].astype(jnp.float32)
    grad_out_low = grad_out.astype(jnp.bfloat16)
    grad_wdown = product(active_low.T, grad_out_low)
    grad_bdown = jnp.sum(grad_out, axis=0)
    (grad_upper,) = gelu_back(product(grad_out_low, wdown.T))
    grad_upper_low = grad_upper.astype(jnp.bfloat16)
    grad_wup = product(normed2.T, grad_upper_low)
    grad_bup = jnp.sum(grad_upper_low.astype(jnp.float32), axis=0)
    grad_normed2 = lax.psum(product(grad_upper_low, wup.T).astype(jnp.bfloat16), "tensor").astype(
        jnp.float32
    )
    grad_norm_in, grad_gain2, grad_shift2 = norm2_back(grad_normed2)
    grad_hidden = grad_out + grad_norm_in
    grad_hidden_low = grad_hidden.astype(jnp.bfloat16)
    grad_bout = jnp.sum(grad_hidden, axis=0)
    grad_wout = product(attended_low.T, grad_hidden_low)
    grad_attended = product(grad_hidden_low, wout.T).astype(jnp.bfloat16)
    grad_heads = grad_attended.reshape(count, local_heads, HEAD)
    again = masked_scores(query_heads, keys_all, key_ok, factor)
    probs_again = jnp.exp(again - log_total)
    probs_low = probs_again.astype(jnp.bfloat16)
    grad_probs = jnp.einsum(
        "qhe,khe->hqk", grad_heads, values_all, preferred_element_type=jnp.float32
    )
    delta = jnp.sum(probs_again * grad_probs, axis=-1, keepdims=True)
    grad_scores = (probs_again * (grad_probs - delta)).astype(jnp.bfloat16)
    grad_queries = (
        (
            jnp.einsum("hqk,khe->qhe", grad_scores, keys_all, preferred_element_type=jnp.float32)
            * factor
        )
        .reshape(count, half)
        .astype(jnp.bfloat16)
    )
    grad_k = (
        jnp.einsum("hqk,qhe->khe", grad_scores, query_heads, preferred_element_type=jnp.float32)
        * factor
    )
    grad_v = jnp.einsum("hqk,qhe->khe", probs_low, grad_heads, preferred_element_type=jnp.float32)
    grad_pairs = lax.psum_scatter(
        jnp.concatenate(
            [
                grad_k.reshape(count * lax.axis_size("ctx"), half),
                grad_v.reshape(count * lax.axis_size("ctx"), half),
            ],
            axis=1,
        ).astype(jnp.bfloat16),
        "ctx",
        scatter_dimension=0,
        tiled=True,
    ).astype(jnp.float32)
    grad_keys = grad_pairs[:, :half].astype(jnp.bfloat16)
    grad_values = grad_pairs[:, half:].astype(jnp.bfloat16)
    grad_normed1 = lax.psum(
        (
            product(grad_queries, wquery.T)
            + product(grad_keys, wkey.T)
            + product(grad_values, wvalue.T)
        ).astype(jnp.bfloat16),
        "tensor",
    ).astype(jnp.float32)
    grad_norm_first, grad_gain1, grad_shift1 = norm1_back(grad_normed1)
    grad_input = (grad_hidden + grad_norm_first)[None]
    grad_wquery = product(normed1.T, grad_queries)
    grad_wkey = product(normed1.T, grad_keys)
    grad_wvalue = product(normed1.T, grad_values)
    grad_bquery = jnp.sum(grad_queries.astype(jnp.float32), axis=0)
    grad_bvalue = jnp.sum(grad_values.astype(jnp.float32), axis=0)
    summed = (
        lax.psum(grad_gain1.astype(jnp.bfloat16), "ctx").astype(jnp.float32),
        lax.psum(grad_shift1.astype(jnp.bfloat16), "ctx").astype(jnp.float32),
        lax.psum(grad_wquery.astype(jnp.bfloat16), "ctx").astype(jnp.float32),
        lax.psum(grad_bquery.astype(jnp.bfloat16), "ctx").astype(jnp.float32),
        lax.psum(grad_wkey.astype(jnp.bfloat16), "ctx").astype(jnp.float32),
        lax.psum(grad_wvalue.astype(jnp.bfloat16), "ctx").astype(jnp.float32),
        lax.psum(grad_bvalue.astype(jnp.bfloat16), "ctx").astype(jnp.float32),
        lax.psum(grad_wout.astype(jnp.bfloat16), "ctx").astype(jnp.float32),
        lax.psum(grad_bout.astype(jnp.bfloat16), "ctx").astype(jnp.float32),
        lax.psum(grad_gain2.astype(jnp.bfloat16), "ctx").astype(jnp.float32),
        lax.psum(grad_shift2.astype(jnp.bfloat16), "ctx").astype(jnp.float32),
        lax.psum(grad_wup.astype(jnp.bfloat16), "ctx").astype(jnp.float32),
        lax.psum(grad_bup.astype(jnp.bfloat16), "ctx").astype(jnp.float32),
        lax.psum(grad_wdown.astype(jnp.bfloat16), "ctx").astype(jnp.float32),
        lax.psum(grad_bdown.astype(jnp.bfloat16), "ctx").astype(jnp.float32),
    )
    owned = (
        lax.psum_scatter(
            summed[0].astype(jnp.bfloat16), "dp", scatter_dimension=0, tiled=True
        ).astype(jnp.float32),
        lax.psum_scatter(
            summed[1].astype(jnp.bfloat16), "dp", scatter_dimension=0, tiled=True
        ).astype(jnp.float32),
        lax.psum_scatter(
            summed[2].astype(jnp.bfloat16), "dp", scatter_dimension=0, tiled=True
        ).astype(jnp.float32),
        lax.psum_scatter(
            summed[3].astype(jnp.bfloat16), "dp", scatter_dimension=0, tiled=True
        ).astype(jnp.float32),
        lax.psum_scatter(
            summed[4].astype(jnp.bfloat16), "dp", scatter_dimension=0, tiled=True
        ).astype(jnp.float32),
        lax.psum_scatter(
            summed[5].astype(jnp.bfloat16), "dp", scatter_dimension=0, tiled=True
        ).astype(jnp.float32),
        lax.psum_scatter(
            summed[6].astype(jnp.bfloat16), "dp", scatter_dimension=0, tiled=True
        ).astype(jnp.float32),
        lax.psum_scatter(
            summed[7].astype(jnp.bfloat16), "dp", scatter_dimension=1, tiled=True
        ).astype(jnp.float32),
        lax.psum_scatter(
            summed[8].astype(jnp.bfloat16), "dp", scatter_dimension=0, tiled=True
        ).astype(jnp.float32),
        lax.psum_scatter(
            summed[9].astype(jnp.bfloat16), "dp", scatter_dimension=0, tiled=True
        ).astype(jnp.float32),
        lax.psum_scatter(
            summed[10].astype(jnp.bfloat16), "dp", scatter_dimension=0, tiled=True
        ).astype(jnp.float32),
        lax.psum_scatter(
            summed[11].astype(jnp.bfloat16), "dp", scatter_dimension=0, tiled=True
        ).astype(jnp.float32),
        lax.psum_scatter(
            summed[12].astype(jnp.bfloat16), "dp", scatter_dimension=0, tiled=True
        ).astype(jnp.float32),
        lax.psum_scatter(
            summed[13].astype(jnp.bfloat16), "dp", scatter_dimension=1, tiled=True
        ).astype(jnp.float32),
        lax.psum_scatter(
            summed[14].astype(jnp.bfloat16), "dp", scatter_dimension=0, tiled=True
        ).astype(jnp.float32),
    )
    return (
        result,
        grad_input,
        owned[0],
        owned[1],
        owned[2],
        owned[3],
        owned[4],
        owned[5],
        owned[6],
        owned[7],
        owned[8],
        owned[9],
        owned[10],
        owned[11],
        owned[12],
        owned[13],
        owned[14],
    )


def solution(mesh):
    placed = (
        P("dp", "ctx", None),
        P("dp"),
        P("dp", "ctx", None),
        P("dp"),
        P("dp"),
        P("dp", "tensor"),
        P(("tensor", "dp")),
        P("dp", "tensor"),
        P("dp", "tensor"),
        P(("tensor", "dp")),
        P("tensor", "dp"),
        P("dp"),
        P("dp"),
        P("dp"),
        P("dp", "tensor"),
        P(("tensor", "dp")),
        P("tensor", "dp"),
        P("dp"),
    )
    return jax.shard_map(
        on_device,
        mesh=mesh,
        in_specs=placed,
        out_specs=(
            P("dp", "ctx", None),
            P("dp", "ctx", None),
            P("dp"),
            P("dp"),
            P("dp", "tensor"),
            P(("tensor", "dp")),
            P("dp", "tensor"),
            P("dp", "tensor"),
            P(("tensor", "dp")),
            P("tensor", "dp"),
            P("dp"),
            P("dp"),
            P("dp"),
            P("dp", "tensor"),
            P(("tensor", "dp")),
            P("tensor", "dp"),
            P("dp"),
        ),
        check_vma=False,
    )
```

profile of v0, /device:TPU:1, one launch (start us, length us, event | category | flops | bytes accessed | tf_op | source)
XLA Modules:
  0.0 577.6 jit_solution(15993076956785587591)
XLA Ops:
  9.9 5.9 %all_gather.51 = bf16[384,192]{1,0:T(8,128)(2,1)S(1)} all-gather(bf16[192,192]{1,0:T(8,128)(2,1)} %param.26), channel_id=1, replica_groups=mesh['dp'=2,'ctx'=32,'tensor'=2] {'dp'}, dimensions={0}, use_global_device_ids=true | all-gather | bytes 221184 | tf_op jit(solution)/shard_map/all_gather | solution.py:80
  21.8 3.8 all-reduce.22
  27.8 4.4 all_gather.50
  36.5 4.3 all_gather.54
  45.8 3.2 all-gather
  50.2 4.5 all_gather.56
  54.7 7.4 %all_gather.60 = bf16[384,768]{1,0:T(8,128)(2,1)} all-gather(bf16[192,768]{1,0:T(8,128)(2,1)S(1)} %copy-done.25), channel_id=1, replica_groups=mesh['dp'=2,'ctx'=32,'tensor'=2] {'dp'}, dimensions={0}, use_global_device_ids=true | all-gather | bytes 884736 | tf_op jit(solution)/shard_map/all_gather | solution.py:86
  62.2 24.6 %all-gather.3.cloned.1.call-done = bf16[4352,384]{1,0:T(8,128)(2,1)} async-done(((bf16[136,384]{1,0:T(8,128)(2,1)}), bf16[4352,384]{1,0:T(8,128)(2,1)}) %all-gather.3.cloned.1.call-update) | async-done | bytes 3342352 | tf_op jit(solution)/shard_map/all_gather | solution.py:108
  86.7 5.5 fusion.77
  92.3 2.9 copy.47
  95.2 3.5 copy.49
  106.5 9.2 %all_gather.62 = bf16[768,384]{0,1:T(8,128)(2,1)S(1)} all-gather(bf16[768,192]{0,1:T(8,128)(2,1)} %param.34), channel_id=1, replica_groups=mesh['dp'=2,'ctx'=32,'tensor'=2] {'dp'}, dimensions={1}, use_global_device_ids=true | all-gather | bytes 884736 | tf_op jit(solution)/shard_map/all_gather | solution.py:88
  115.8 20.0 %all-reduce.29.cloned.1.call-done = f32[136,384]{1,0:T(8,128)} async-done(((f32[136,384]{1,0:T(8,128)}), f32[136,384]{1,0:T(8,128)}) %all-reduce.29.cloned.1.call-update) | async-done | bytes 208912 | tf_op jit(solution)/shard_map/psum | solution.py:124
  141.1 28.4 %all-reduce.31.cloned.1.call-done = bf16[136,384]{1,0:T(8,128)(2,1)} async-done(((bf16[136,384]{1,0:T(8,128)(2,1)}), bf16[136,384]{1,0:T(8,128)(2,1)}) %all-reduce.31.cloned.1.call-update) | async-done | bytes 104464 | tf_op jit(solution)/shard_map/psum | solution.py:142
  175.0 8.0 %multiply_reduce_fusion = (f32[3,136]{1,0:T(4,128)S(1)}, f32[3,136,4352]{2,1,0:T(8,128)}) fusion(f32[3,136,4352]{2,1,0:T(8,128)} %copy-done, f32[3,136]{1,0:T(4,128)S(1)} %log_add_fusion, bf16[136,3,64]{0,2,1:T(8,128)(2,1)S(1)} %bitcast.129, bf16[4352,3,64]{0,2,1:T(8,128)(2,1)} %bitcast.124), kind=kOutput, calls=%fused_computation.3 | convolution fusion | flops 232605280 | bytes 15931584 | tf_op jit(solution)/shard_map/qhe,khe->hqk/dot_general | solution.py:155
  184.5 4.7 multiply_convert_fusion
  201.5 3.5 bitcast_reduce_fusion
  205.8 97.2 %all-reduce.33.cloned.1.call-done = bf16[4352,384]{0,1:T(8,128)(2,1)} async-done(((bf16[4352,384]{0,1:T(8,128)(2,1)}), bf16[4352,384]{0,1:T(8,128)(2,1)}) %all-reduce.33.cloned.1.call-update) | async-done | bytes 3342352
  316.7 2.5 reduce-scatter.20.cloned.1.call-done
  324.0 29.6 %all-reduce.37.cloned.1.call-done = (bf16[136,384]{1,0:T(8,128)(2,1)}, bf16[136,384]{1,0:T(8,128)(2,1)}) async-done(((bf16[136,384]{1,0:T(8,128)(2,1)}, bf16[136,384]{1,0:T(8,128)(2,1)}), (bf16[136,384]{1,0:T(8,128)(2,1)}, bf16[136,384]{1,0:T(8,128)(2,1)})) %all-reduce.37.cloned.1.call-update) | async-done | bytes 208912 | tf_op jit(solution)/shard_map/psum | solution.py:132
  356.9 5.3 all-reduce.21
  362.9 66.1 %all-reduce.18 = (bf16[192]{0:T(256)(128)(2,1)S(1)}, bf16[192]{0:T(256)(128)(2,1)S(1)}, bf16[96]{0:T(256)(128)(2,1)S(1)}, bf16[96]{0:T(256)(128)(2,1)S(1)}, bf16...) all-reduce(bf16[192]{0:T(256)(128)(2,1)S(1)} %dynamic-slice.11, ...), channel_id=1, replica_groups=mesh['dp'=2,'ctx'=32,'tensor'=2] {'ctx'}, use_global_device_ids=true, to_apply=%region_17.18 | all-reduce | flops 1728 | bytes 6912 | tf_op jit(solution)/shard_map/psum | solution.py:203
  435.6 13.1 %reduce-scatter.14.cloned.1.call-done = bf16[192,192]{1,0:T(8,128)(2,1)} async-done(((bf16[384,192]{1,0:T(8,128)(2,1)}), bf16[192,192]{1,0:T(8,128)(2,1)}) %reduce-scatter.14.cloned.1.call-update) | async-done | bytes 73744 | tf_op jit(solution)/shard_map/reduce_scatter | solution.py:235
  450.5 110.3 %all-reduce.35.cloned.1.call-done = (bf16[192,192]{1,0:T(8,128)(2,1)}, bf16[192,192]{1,0:T(8,128)(2,1)}, bf16[192,192]{1,0:T(8,128)(2,1)}, bf16[192,192]{1,0:T(8...) async-done(((bf16[192,192]{1,0:T(8,128)(2,1)}, bf16[192,192]{1,0:T(8,128)(2,1)}, bf16[192,192]{1,0:T(8,128)(2,1)}, bf16[192,192]{1,0:T(8,128)(2,1)}, ...) | async-done | bytes 884752 | tf_op jit(solution)/shard_map/psum | solution.py:205
  (240 shorter events, 90.0 us)
Async XLA Ops:
  7.2 79.5 %all-gather.3.cloned.1.call-start = ((), (), s32[]{:S(2)}) async-start(), calls=%async_computation.6 | async-start | bytes 3446784 | tf_op jit(solution)/shard_map/all_gather | solution.py:108
  35.9 99.8 %all-reduce.29.cloned.1.call-start = ((), (), s32[]{:S(2)}) async-start(), calls=%async_computation.7 | async-start | bytes 417792 | tf_op jit(solution)/shard_map/psum | solution.py:124
  106.4 63.1 %all-reduce.31.cloned.1.call-start = ((), (), s32[]{:S(2)}) async-start(), calls=%async_computation.8 | async-start | bytes 208896 | tf_op jit(solution)/shard_map/psum | solution.py:142
  140.9 162.1 %all-reduce.33.cloned.1.call-start = ((), (), s32[]{:S(2)}) async-start(), calls=%async_computation.15 | async-start | bytes 6684672
  193.7 125.5 %reduce-scatter.20.cloned.1.call-start = ((), (), s32[]{:S(2)}) async-start(), calls=%async_computation.14 | async-start | bytes 294912
  205.0 105.9 %copy-start.37 = (f32[136]{0:T(256)S(1)}, f32[136]{0:T(256)}, u32[]{:S(2)}) copy-start(f32[136]{0:T(256)} %copy-done.36) | copy-start | bytes 1636
  205.0 107.2 %copy-start.8 = (bf16[1,136,384]{2,1,0:T(8,128)(2,1)S(1)}, bf16[1,136,384]{2,1,0:T(8,128)(2,1)}, u32[]{:S(2)}) copy-start(bf16[1,136,384]{2,1,0:T(8,128)(2,1)} %param.18) | copy-start | bytes 313348
  205.1 107.2 %copy-start.28 = (f32[384]{0:T(512)S(1)}, f32[384]{0:T(512)}, u32[]{:S(2)}) copy-start(f32[384]{0:T(512)} %copy-done.27) | copy-start | bytes 4612
  205.1 107.2 %copy-start.30 = (f32[136]{0:T(256)S(1)}, f32[136]{0:T(256)}, u32[]{:S(2)}) copy-start(f32[136]{0:T(256)} %copy-done.29) | copy-start | bytes 1636
  205.1 107.2 %copy-start.33 = (f32[136]{0:T(256)S(1)}, f32[136]{0:T(256)}, u32[]{:S(2)}) copy-start(f32[136]{0:T(256)} %copy-done.32) | copy-start | bytes 1636
  205.1 107.2 %copy-start.46 = (f32[384]{0:T(512)S(1)}, f32[384]{0:T(512)}, u32[]{:S(2)}) copy-start(f32[384]{0:T(512)} %copy-done.45) | copy-start | bytes 4612
  205.1 111.2 %copy-start.48 = (bf16[192]{0:T(256)(128)(2,1)S(1)}, bf16[192]{0:T(256)(128)(2,1)}, u32[]{:S(2)}) copy-start(bf16[192]{0:T(256)(128)(2,1)} %param.35) | copy-start | bytes 1156
  205.1 111.5 %copy-start.47 = (bf16[3,64]{1,0:T(4,128)(2,1)S(1)}, bf16[3,64]{1,0:T(4,128)(2,1)}, u32[]{:S(2)}) copy-start(bf16[3,64]{1,0:T(4,128)(2,1)} %get-tuple-element.71) | copy-start | bytes 1156
  205.1 111.5 %copy-start.13 = (bf16[136,384]{1,0:T(8,128)(2,1)S(1)}, bf16[136,384]{1,0:T(8,128)(2,1)}, u32[]{:S(2)}) copy-start(bf16[136,384]{1,0:T(8,128)(2,1)} %all-reduce.31.cloned.1.call-done) | copy-start | bytes 313348
  205.7 149.1 %copy-start.35 = (f32[136]{0:T(256)S(1)}, f32[136]{0:T(256)}, u32[]{:S(2)}) copy-start(f32[136]{0:T(256)} %copy-done.34) | copy-start | bytes 1636
  205.7 147.9 %all-reduce.37.cloned.1.call-start = ((), (), s32[]{:S(2)}) async-start(), calls=%async_computation.17 | async-start | bytes 417792 | tf_op jit(solution)/shard_map/psum | solution.py:132
  304.3 129.7 %copy-start.5 = (f32[136,384]{1,0:T(8,128)S(1)}, f32[136,384]{1,0:T(8,128)}, u32[]{:S(2)}) copy-start(f32[136,384]{1,0:T(8,128)} %copy-done.4) | copy-start | bytes 626692
  306.4 129.2 %reduce-scatter.10.cloned.1.call-start = ((), (), s32[]{:S(2)}) async-start(), calls=%async_computation.9 | async-start | bytes 294912 | tf_op jit(solution)/shard_map/reduce_scatter | solution.py:226
  308.4 140.3 %copy-start.10 = (f32[136,384]{1,0:T(8,128)S(1)}, f32[136,384]{1,0:T(8,128)}, u32[]{:S(2)}) copy-start(f32[136,384]{1,0:T(8,128)} %copy-done.9) | copy-start | bytes 626692
  308.5 127.2 %reduce-scatter.16.cloned.1.call-start = ((), (), s32[]{:S(2)}) async-start(), calls=%async_computation.12 | async-start | bytes 884736 | tf_op jit(solution)/shard_map/reduce_scatter | solution.py:253
  310.9 124.7 %reduce-scatter.18.cloned.1.call-start = ((), (), s32[]{:S(2)}) async-start(), calls=%async_computation.13 | async-start | bytes 884736 | tf_op jit(solution)/shard_map/reduce_scatter | solution.py:259
  312.2 123.4 %reduce-scatter.12.cloned.1.call-start = ((), (), s32[]{:S(2)}) async-start(), calls=%async_computation.10 | async-start | bytes 294912 | tf_op jit(solution)/shard_map/reduce_scatter | solution.py:232
  314.3 134.4 %reduce-scatter.14.cloned.1.call-start = ((), (), s32[]{:S(2)}) async-start(), calls=%async_computation.11 | async-start | bytes 294912 | tf_op jit(solution)/shard_map/reduce_scatter | solution.py:235
  322.9 237.9 %all-reduce.35.cloned.1.call-start = ((), (), s32[]{:S(2)}) async-start(), calls=%async_computation.16 | async-start | bytes 1966080 | tf_op jit(solution)/shard_map/psum | solution.py:205
  (39 other events, 1108.9 us)
Sparse Core Ops, SparseCore 0:
  36.0 50.6 all-gather.2
  106.6 29.1 all-reduce.28
  141.0 28.4 all-reduce.30
  193.8 109.0 all-reduce.32
  305.8 13.3 reduce-scatter.19
  322.3 31.2 all-reduce.36
  356.7 13.2 reduce-scatter.9
  373.0 18.8 reduce-scatter.15
  394.8 18.8 reduce-scatter.17
  416.6 14.4 reduce-scatter.11
  434.2 14.4 reduce-scatter.13
  453.7 107.0 all-reduce.34
where the time goes:
time: 579 us; the launch traced here: 578 us
  waiting for transfers between devices  326 us (56%)
  blocking collectives  114 us (20%)
  matrix products  42.9 us (7%)
  other arithmetic  40.3 us (7%)
  local copies, waits for them, and re-layouts  34.2 us (6%)
  between operations  19.5 us (3%)
    psum x1, waiting for transfers between devices, on_device(): lax.psum(grad_wquery.astype(jnp.bfloat16), 'ctx').astype(jnp.float32)  110 us
    unnamed x14, waiting for transfers between devices  99.9 us
    psum x1, blocking collectives, on_device(): lax.psum(grad_gain1.astype(jnp.bfloat16), 'ctx').astype(jnp.float32)  66.1 us
    psum x1, waiting for transfers between devices, on_device(): lax.psum(product(active_low, wdown).astype(jnp.bfloat16), 'tensor')  29.6 us
    psum x1, waiting for transfers between devices, on_device(): lax.psum(product(grad_upper_low, wup.T).astype(jnp.bfloat16), 'tensor')  28.4 us
    dot_general x18, matrix products, product(): return jnp.dot(left, right, preferred_element_type=jnp.float32)  25.3 us
    all_gather x1, waiting for transfers between devices, on_device(): lax.all_gather(jnp.concatenate([keys_own, values_own], axis=1), 'ctx', ax...  24.6 us
    unnamed x133, local copies, waits for them, and re-layouts  20.7 us
  transfers between devices with their start and end apart: 12, of which 8 were waited for; matrix products, arithmetic and copies ran while one was open for 8% of the time, Pallas kernels for 0%

commit v1 on v0

v1 whole, which is shorter than its diff:
```python
import jax
import jax.numpy as jnp
from jax import lax
from jax.experimental import pallas as pl
from jax.experimental.pallas import tpu as pltpu
from jax.sharding import PartitionSpec as P

F32 = jnp.float32
BF16 = jnp.bfloat16
MESH = pl.DeviceIdType.MESH

HEAD = 64
OWN = 136
PAD = 144
WIDE = 384
HALF = 192
HID = 768
GROUP = 4 * PAD
STACK = 3 * PAD
EPSILON = 1e-06
UNITS_1 = 80
UNITS_2 = 32
UNITS_3 = 16
NORM_ROWS = 864
COPIES = 288
VMEM_BYTES = 63 * 1024 * 1024
SMALL = (HALF, HALF, HALF, HALF, HALF, HALF, 96, 96, WIDE)


def mm(left, right):
    return lax.dot_general(left, right, (((1,), (0,)), ((), ())), preferred_element_type=F32)


def mm_nt(left, right):
    return lax.dot_general(left, right, (((1,), (1,)), ((), ())), preferred_element_type=F32)


def mm_tn(left, right):
    return lax.dot_general(left, right, (((0,), (0,)), ((), ())), preferred_element_type=F32)


def rows(start, size):
    return pl.ds(pl.multiple_of(start, 16), size)


def lanes_of(shape):
    return lax.broadcasted_iota(jnp.int32, shape, 1)


def widen(value):
    return jnp.concatenate([value, jnp.zeros((value.shape[0], 64), value.dtype)], axis=1)


def three_parts(value):
    high = value.astype(BF16).astype(F32)
    rest = value - high
    middle = rest.astype(BF16).astype(F32)
    return high, middle, (rest - middle).astype(BF16).astype(F32)


def layer_kernel(
    x_ref, count_ref, cot_ref, g1_ref, s1_ref, wq_ref, bq_ref, wk_ref, wv_ref, bv_ref, wo_ref, bo_ref,
    g2_ref, s2_ref, wu_ref, bu_ref, wd_ref, bd_ref,
    y_ref, gx_ref, f1_ref, f2_ref, f3_ref,
    send_sems, recv_sems, load_sems,
    wqf, wkf, wvf, wof, wuf, wdt, woc, vec, vfull, xin, cotin, *rest_refs
):
    small_refs, rest_refs = rest_refs[: len(SMALL)], rest_refs[len(SMALL) :]
    (
    kvx, qx, nkv, nq, dob, picker, wall, wall_t, qall, qbig, kbuf, vbuf, kt, vt, bias, pt, mrow, om, omr, dobig, factor, gscore, acck, accv, dqm, dqr,
    gsib, gsibr, gown, gy, gyr,
    xh1, rstd1, n1, gout, attf, attx, hid, xh2, rstd2, n2, act, gup, gn2p, gn1x, ghid, gnq,
    src1, sib1, s01, ar1, s11, br1, fin1,
    src2, sib2, s02, all2, fin2, src3, sib3, s03, all3, fin3, tr2, yout, gxout,
    ) = rest_refs
    d, n, t = lax.axis_index("dp"), lax.axis_index("ctx"), lax.axis_index("tensor")
    c, chip = n % 2, n // 2
    chip_x, chip_y = chip // 4, chip % 4
    a, b = chip_x * (1 - c) + chip_y * c, chip_y * (1 - c) + chip_x * c

    def dev(to_a, to_b):
        to_x, to_y = to_a * (1 - c) + to_b * c, to_b * (1 - c) + to_a * c
        return (d, (to_x * 4 + to_y) * 2 + c, t)

    d_other, t_other = 1 - d, 1 - t
    sib = (d, n + 1 - 2 * c, t)
    z_dp, z_tensor, z_both = (d_other, n, t), (d, n, t_other), (d_other, n, t_other)
    a_up, a_down, a_far = (a + 1) % 4, (a + 3) % 4, (a + 2) % 4
    b_up, b_down, b_far = (b + 1) % 4, (b + 3) % 4, (b + 2) % 4

    def by_place(to_x, to_y):
        return (d, (to_x * 4 + to_y) * 2 + c, t)

    xs = [chip_x, (chip_x + 3) % 4, (chip_x + 1) % 4, (chip_x + 2) % 4]
    ys = [chip_y, (chip_y + 3) % 4, (chip_y + 1) % 4, (chip_y + 2) % 4]
    x_dev, y_dev = [by_place(x, chip_y) for x in xs], [by_place(chip_x, y) for y in ys]

    barrier = pltpu.get_barrier_semaphore()
    a_plus, a_minus, b_plus, b_minus = dev(a_up, b), dev(a_down, b), dev(a, b_up), dev(a, b_down)
    a_across, b_across = dev(a_far, b), dev(a, b_far)
    along_a = ((a_up, a_plus), (a_far, a_across), (a_down, a_minus))
    along_b = ((b_up, b_plus), (b_far, b_across), (b_down, b_minus))
    other_plane = [(d_other, device[1], t) for device in (z_dp, b_plus, b_across, b_minus)]
    tensor_sib = (d, sib[1], t_other)
    everywhere = [
        (plane, place, (d, d_other)[plane], dev(place[0], place[1]))
        for plane in range(2)
        for place in [(to_a, to_b) for to_a in (a, a_up, a_far, a_down) for to_b in (b, b_up, b_far, b_down)]
    ][1:]
    everywhere = [(i + 1, plane, place, (to_d, device[1], t)) for i, (plane, place, to_d, device) in enumerate(everywhere)]
    partners = [sib, z_tensor, z_both, tensor_sib] + [device for _, _, _, device in everywhere]
    for partner in partners:
        pl.semaphore_signal(barrier, inc=1, device_id=partner, device_id_type=MESH)

    sent = []

    class Copy:
        def __init__(self, source, target, device, k=None):
            self.parts = source, target, device
            self.k = k
            if k is None:
                self.k = len(sent)
                sent.append(self)
            self.made().start()

        def made(self):
            source, target, device = (part() if callable(part) else part for part in self.parts)
            return pltpu.make_async_remote_copy(
                src_ref=source, dst_ref=target, send_sem=send_sems.at[self.k], recv_sem=recv_sems.at[self.k],
                device_id=device, device_id_type=MESH,
            )

        def wait_recv(self):
            self.made().wait_recv()

        def wait_send(self):
            self.made().wait_send()

    def send(source, target, device):
        return Copy(source, target, device)

    def send_all(pieces, like):
        first = Copy(*pieces[0])
        for piece in pieces[1:]:
            Copy(*piece, k=first.k)
        first.parts = like, like, first.parts[2]
        return first

    gone = [0]

    def flush(mark):
        for copy in sent[gone[0] : mark]:
            copy.wait_send()
        gone[0] = mark

    loads = []

    def load(source, target):
        copy = pltpu.make_async_copy(source, target, load_sems.at[len(loads)])
        copy.start()
        loads.append(copy)
        return copy

    x_load = load(x_ref, xin)
    small_in = (g1_ref, s1_ref, bo_ref, g2_ref, s2_ref, bd_ref, bq_ref, bv_ref, bu_ref)
    small_loads = [load(source, target) for source, target in zip(small_in, small_refs)]
    own_rows = rows(d * HALF, HALF)
    qkv_loads = [load(ref, full.at[own_rows]) for ref, full in ((wv_ref, wvf), (wk_ref, wkf), (wq_ref, wqf))]
    cot_load = load(cot_ref, cotin)
    ff_loads = [load(wu_ref, wuf.at[t, own_rows]), load(wd_ref, wdt.at[t, own_rows]), load(wo_ref, wof.at[t, d])]
    limit = count_ref[0]
    x_load.wait()
    tokens = jnp.concatenate([xin[0].astype(F32), jnp.zeros((PAD - OWN, WIDE), F32)], axis=0)
    kvx[c, chip_y] = tokens.astype(BF16)
    qx[chip_x] = tokens.astype(BF16)
    vec[t, d] = jnp.zeros((16, WIDE), F32)
    for i, (copy, ref, size) in enumerate(zip(small_loads, small_refs, SMALL)):
        copy.wait()
        vec[t, d, i : i + 1, 0:size] = jnp.reshape(ref[...].astype(F32), (1, size))

    pl.semaphore_wait(barrier, len(partners))

    def ring(view, places, devices):
        cuts = pl.ds(0, 80), pl.ds(80, 64)
        own, down, up, _ = places
        _, minus, plus, _ = devices
        going = {}

        def put(i, half, device):
            return send(lambda: view(i, cuts[half]), lambda: view(i, cuts[half]), device)

        def start():
            for half in range(2):
                for way, device in enumerate((plus, minus)):
                    going[half, way] = put(own, half, device)

        def near():
            for half in range(2):
                going[half, half].wait_recv()
                going["far", half] = put((down, up)[half], half, (plus, minus)[half])
            for half in range(2):
                going[half, 1 - half].wait_recv()

        def last():
            for half in range(2):
                going["far", half].wait_recv()

        return start, near, last

    kv_start, kv_near, kv_last = ring(lambda i, cut: kvx.at[c, i, cut], ys, y_dev)
    qx_start, qx_near, qx_last = ring(lambda i, cut: qx.at[i, cut], xs, x_dev)
    do_start, do_near, do_last = ring(lambda i, cut: dob.at[i, cut], xs, x_dev)

    def share(i):
        return send(lambda: kvx.at[c, i], lambda: kvx.at[c, i], sib)

    kv_start()
    shares = [share(ys[0])]
    qx_start()
    vec_copies = [send(vec.at[t, d], vec.at[t, d], device) for device in (z_dp, z_tensor, z_both)]
    part = rows(c * 96, 96)
    first = [
        (full, send(ref.at[part], full.at[rows(d * HALF + c * 96, 96)], z_dp))
        for ref, full in ((wv_ref, wvf), (wk_ref, wkf), (wq_ref, wqf))
    ]
    def at_part(full, to_t, to_d, first=0, size=96):
        if full is wof:
            return full.at[to_t, to_d, rows(c * 96 + first, size)]
        return full.at[to_t, rows(to_d * HALF + c * 96 + first, size)]

    def move(full, to_t, to_d, first, size, device):
        def view():
            return at_part(full, to_t, to_d, first, size)

        return send(view, view, device)

    out_copies = [send(wo_ref.at[part], at_part(wof, t, d), device) for device in (z_dp, z_both, z_tensor)]
    by_dp, by_both, relayed, handed = {}, {}, {}, {}
    for name, ref, full in (("up", wu_ref, wuf), ("down", wd_ref, wdt)):
        by_dp[name] = full, send(ref.at[part], at_part(full, t, d), z_dp)
        by_both[name] = full, send(ref.at[part], at_part(full, t, d), z_both)

    def hand_out():
        for copy in out_copies:
            copy.wait_recv()
        handed["out"] = [
            move(wof, to_t, to_d, 0, 96, sib) for to_t, to_d in ((t, d_other), (t_other, d_other), (t_other, d))
        ]

    def relay(name):
        full, copy = by_dp[name]
        copy.wait_recv()
        relayed[name] = [move(full, t, d_other, 0, 48, z_both)]
        handed[name] = [move(full, t, d_other, 0, 96, sib)]
        _, copy = by_both[name]
        copy.wait_recv()
        relayed[name].append(move(full, t_other, d_other, 48, 48, z_dp))
        handed[name, "far"] = [move(full, t_other, d_other, 0, 96, sib)]

    def hand_relayed(name):
        for copy in relayed[name]:
            copy.wait_recv()
        handed[name, "far"].append(move(by_dp[name][0], t_other, d, 0, 96, sib))

    def have(*names):
        for name in names:
            for copy in handed[name]:
                copy.wait_recv()

    center = tokens - jnp.mean(tokens, axis=1, keepdims=True)
    scale = lax.rsqrt(jnp.mean(center * center, axis=1, keepdims=True) + EPSILON)
    xh1[...] = center * scale
    rstd1[...] = scale
    row = lax.broadcasted_iota(jnp.int32, (PAD, 1), 0)
    own_ok = (row < OWN) & (n * OWN + row < limit)
    cot_load.wait()
    cot = jnp.concatenate([cotin[0].astype(F32), jnp.zeros((PAD - OWN, WIDE), F32)], axis=0)
    gout[...] = jnp.where(own_ok, cot, 0.0)
    for half, core in enumerate((c, 1 - c)):
        for y in range(4):
            where = (chip_x * 4 + y) * 2 + core
            ok = (row < OWN) & (where * OWN + row < limit)
            bias[half, pl.ds(y * PAD, PAD), :] = jnp.where(ok, 0.0, -1e30)

    def normed_of(tokens):
        ones = jnp.full((WIDE, 128), 1.0, BF16)
        mean = mm(tokens, ones) * (1.0 / WIDE)
        center = tokens.astype(F32) - jnp.concatenate([mean] * 3, axis=1)
        scale = lax.rsqrt(mm((center * center).astype(BF16), ones) * (1.0 / WIDE) + EPSILON)
        return (center * jnp.concatenate([scale] * 3, axis=1) * gain1 + shift1).astype(BF16)

    kv_near()
    shares += [share(ys[1]), share(ys[2])]
    qx_near()
    vec_copies[0].wait_recv()
    vfull[...] = vec[t, 0] + pltpu.roll(vec[t, 1], HALF, 1)
    bias_half = vec[t, 0] + pltpu.roll(vec[t, 1], 96, 1)
    gain1, shift1 = vfull[0:1, :], vfull[1:2, :]
    normed1 = (xh1[...] * gain1 + shift1).astype(BF16)
    n1[...] = normed1
    nkv[0, ys[0]] = normed1
    nq[xs[0]] = normed1
    for j in (1, 2):
        nkv[0, ys[j]] = normed_of(kvx[c, ys[j]])
        nq[xs[j]] = normed_of(qx[xs[j]])
    second = []
    for full, copy in first:
        copy.wait_recv()

        def half_of(full=full):
            return full.at[rows(d_other * HALF + c * 96, 96)]

        second.append(send(half_of, half_of, sib))
    for copy in qkv_loads:
        copy.wait()
    kv_last()
    shares.append(share(ys[3]))
    nkv[0, ys[3]] = normed_of(kvx[c, ys[3]])
    qx_last()
    nq[xs[3]] = normed_of(qx[xs[3]])
    for copy in second:
        copy.wait_recv()
    for i, full in enumerate((wkf, wvf, wqf)):
        wall[i] = widen(full[...].astype(F32)).astype(BF16)
    for i in range(2):
        wall_t[i] = jnp.transpose(widen((wkf, wvf)[i][...].astype(F32))).astype(BF16)
    lane = lanes_of((PAD, 256))
    tile_lane = lanes_of((PAD, 128))
    wide_lane = lanes_of((GROUP, 256))
    ones_v = jnp.where((lanes_of((1, 256)) >= HALF) & (lanes_of((1, 256)) < HALF + 9), 1.0, 0.0)
    bias_v = jnp.where(lanes_of((1, 256)) < HALF, bias_half[7:8, 0:256], 0.0)
    bias_q = jnp.where(lanes_of((1, 256)) < HALF, bias_half[6:7, 0:256], 0.0)
    bias_v_t = jnp.transpose(jnp.broadcast_to(bias_v + ones_v, (128, 256)))[:, 0:1]

    def head_lanes(h):
        return (lane >= 64 * h) & (lane < 64 + 64 * h)

    query = (mm(nq[...].reshape(GROUP, WIDE), wall[2]) + bias_q).astype(BF16)
    qall[...] = query.reshape(4, PAD, 256)
    for j in range(4):
        query = qall[xs[j]].astype(F32) * 0.125
        for h in range(3):
            qbig[j, pl.ds(h * PAD, PAD), :] = jnp.where(
                head_lanes(h), query, jnp.where(lane == HALF, 1.0, 0.0)
            ).astype(BF16)

    def project(half):
        normed = nkv[half].reshape(GROUP, WIDE)
        kbuf[pl.ds(half * GROUP, GROUP), :] = jnp.where(
            wide_lane == HALF, bias[half], mm(normed, wall[0])
        ).astype(BF16)
        vbuf[pl.ds(half * GROUP, GROUP), :] = (mm(normed, wall[1]) + (bias_v + ones_v)).astype(BF16)
        kt[half] = mm_nt(wall_t[0], normed).astype(BF16)
        vt[half] = (mm_nt(wall_t[1], normed) + bias_v_t).astype(BF16)

    project(0)
    for j in range(4):
        shares[j].wait_recv()
        nkv[1, ys[j]] = normed_of(kvx[1 - c, ys[j]])
    project(1)

    across = lanes_of((PAD, STACK)) - lax.broadcasted_iota(jnp.int32, (PAD, STACK), 0)
    picker[...] = jnp.where((across == 0) | (across == PAD) | (across == 2 * PAD), 1.0, 0.0).astype(BF16)

    def head_of_column(shape):
        column = lanes_of(shape)
        return (column >= PAD).astype(jnp.int32) + (column >= 2 * PAD).astype(jnp.int32)

    def own_head(value):
        down = lax.broadcasted_iota(jnp.int32, (HALF, STACK), 0)
        return jnp.where(((down >= 64).astype(jnp.int32) + (down >= 128).astype(jnp.int32)) == head_of_column((HALF, STACK)), value, 0.0)

    def parts_block(line):
        down = lax.broadcasted_iota(jnp.int32, (16, STACK), 0)
        head = (down >= 3).astype(jnp.int32) + (down >= 6).astype(jnp.int32)
        high, middle, rest = three_parts(line)
        i = down - 3 * head
        value = jnp.where(i == 0, high, jnp.where(i == 1, middle, rest))
        return jnp.where((head == head_of_column((16, STACK))) & (down < 9), value, 0.0)

    def times(left, right):
        return mm(left[0], right[0:GROUP]) + mm(left[1], right[GROUP:])

    def forward(j):
        scores = mm_nt(kbuf[...], qbig[j])
        top = jnp.max(scores, axis=0, keepdims=True)
        low = jnp.exp(scores - top).astype(BF16)
        pt[j] = low
        mrow[j] = top
        mixed = times([vt[i, 0:208, :] for i in range(2)], low)
        total = mixed[HALF : HALF + 1, :]
        whole = [own_head(mixed[0:HALF] * (1.0 / total)), parts_block(top), parts_block(total), jnp.zeros((32, STACK), F32)]
        om[j] = mm_nt(picker[...], jnp.concatenate(whole, axis=0).astype(BF16)).astype(BF16)

    partial = {}

    def send_partial(j):
        partial[j] = send(lambda: om.at[j], lambda: omr.at[j - 1], x_dev[j])

    @pl.loop(0, 4)
    def _(i):
        forward(3 - i)

        @pl.when(i == 0)
        def _():
            send_partial(3)
            hand_out()
            relay("up")

        @pl.when(i == 1)
        def _():
            send_partial(2)
            relay("down")

        @pl.when(i == 2)
        def _():
            send_partial(1)

    x_mark = len(sent)
    for j in (3, 2, 1):
        partial[j].wait_recv()
    messages = [om[0].astype(F32)] + [omr[j].astype(F32) for j in range(3)]
    tops, sums = [], []
    for message in messages:
        tile = message[:, 128:256]
        tile = tile + pltpu.roll(tile, 127, 1) + pltpu.roll(tile, 126, 1)
        tops.append(tile)
        sums.append(pltpu.roll(tile, 112, 1))
    top = jnp.maximum(jnp.maximum(tops[0], tops[1]), jnp.maximum(tops[2], tops[3]))
    parts = [jnp.exp(own - top) * total for own, total in zip(tops, sums)]
    total = parts[0] + parts[1] + parts[2] + parts[3]
    over = 1.0 / total
    lse = top + jnp.log(total)
    attended = jnp.zeros((PAD, 256), F32)
    for message, own in zip(messages, parts):
        ratio = own * over
        spread = jnp.where(lane < 64, ratio[:, 64:65], jnp.where(lane < 128, ratio[:, 67:68], ratio[:, 70:71]))
        attended = attended + message * spread
    attended = jnp.where(lane < HALF, attended, 0.0)
    attf[...] = attended
    attx[t] = attended[:, 0:HALF].astype(BF16)
    att_copy = send(attx.at[t], attx.at[t], z_tensor)
    hand_relayed("up")
    hand_relayed("down")
    have("out", "up", "down")
    for copy in ff_loads:
        copy.wait()
    for copy in vec_copies[1:]:
        copy.wait_recv()
    for i in range(2):
        woc[i] = jnp.concatenate([wof[i, 0], wof[i, 1]], axis=1)
    grad_low = gout[...].astype(BF16)
    valid = (tile_lane == 64) | (tile_lane == 67) | (tile_lane == 70)
    high, middle, rest = three_parts(jnp.where(valid, lse, 0.0))
    stats = pltpu.roll(high, 16, 1) + pltpu.roll(middle, 17, 1) + pltpu.roll(rest, 18, 1)
    flush(x_mark)
    att_copy.wait_recv()

    tokens = jnp.concatenate([xin[0].astype(F32), jnp.zeros((PAD - OWN, WIDE), F32)], axis=0)
    hidden1 = tokens + (mm(attx[0], woc[0]) + mm(attx[1], woc[1])) + vfull[2:3, :]
    hid[...] = hidden1
    center = hidden1 - jnp.mean(hidden1, axis=1, keepdims=True)
    scale = lax.rsqrt(jnp.mean(center * center, axis=1, keepdims=True) + EPSILON)
    xhat2 = center * scale
    xh2[...] = xhat2
    rstd2[...] = scale
    n2[...] = (xhat2 * vfull[3:4, :] + vfull[4:5, :]).astype(BF16)

    @pl.loop(0, 2)
    def _(step):
        i = t + step * (1 - 2 * t)

        @pl.when(step == 1)
        def _():
            have(("up", "far"), ("down", "far"))

        bias_up = jnp.concatenate([vec[i, 0, 8:9, :], vec[i, 1, 8:9, :]], axis=1)
        upper = mm(n2[...], wuf[i]) + bias_up
        gate = 0.5 + 0.5 * lax.erf(upper * 0.7071067811865476)
        act[i] = (upper * gate).astype(BF16)
        slope = gate + upper * jnp.exp(upper * upper * -0.5) * 0.3989422804014327
        gup[i] = (mm(grad_low, wdt[i]) * slope).astype(BF16)
        gn2p[i] = mm_nt(gup[i], wuf[i])

    grad_n2 = gn2p[0] + gn2p[1]

    xhat2 = xh2[...]
    z = grad_n2 * vfull[3:4, :]
    mean_z = jnp.mean(z, axis=1, keepdims=True)
    mean_zx = jnp.mean(z * xhat2, axis=1, keepdims=True)
    grad_h = gout[...] + (z - mean_z - xhat2 * mean_zx) * rstd2[...]
    ghid[...] = grad_h
    grad_h_low = grad_h.astype(BF16)
    grad_att = mm_nt(grad_h_low, woc[t]).astype(BF16)
    grad_att_w = widen(grad_att).astype(F32)
    product = grad_att_w * attf[...]
    message = jnp.where(tile_lane < 64, grad_att_w[:, 128:256], stats)
    for h in range(3):
        delta = jnp.sum(jnp.where(head_lanes(h), product, 0.0), axis=1, keepdims=True)
        for i, piece in enumerate(three_parts(delta)):
            message = jnp.where(tile_lane == 64 + 3 * h + i, -piece, message)
    dob[chip_x] = jnp.concatenate([grad_att_w[:, 0:128], message], axis=1).astype(BF16)
    do_start()
    def put_tiles(buf, dp, at, tall):
        r = tall.shape[0]
        buf[dp, pl.ds(at, r), :] = tall[:, 0:128].astype(BF16)
        tail = jnp.concatenate([tall[0 : r // 2, 128:HALF], tall[r // 2 :, 128:HALF]], axis=1)
        buf[dp, pl.ds(at + r, r // 2), :] = tail.astype(BF16)

    def put_rows(buf, at, pieces):
        for dp in range(2):
            lines = []
            for pair in pieces:
                line = pair[dp]
                size = line.shape[1]
                for i in range(0, size, 128):
                    piece = line[:, i : min(i + 128, size)]
                    if piece.shape[1] < 128:
                        piece = jnp.concatenate([piece, jnp.zeros((1, 128 - piece.shape[1]), F32)], axis=1)
                    lines.append(piece)
            lines.append(jnp.zeros((16 - len(lines), 128), F32))
            buf[dp, pl.ds(at, 16), :] = jnp.concatenate(lines, axis=0).astype(BF16)

    def halves(line):
        size = line.shape[1] // 2
        return line[:, 0:size], line[:, size:]

    def column_sum(value):
        return jnp.sum(value, axis=0, keepdims=True)

    def put_wide(buf, at, whole):
        for dp in range(2):
            for i in range(6):
                buf[dp, pl.ds(at + i * HALF, HALF), :] = whole[
                    dp * HALF : (dp + 1) * HALF, i * 128 : (i + 1) * 128
                ].astype(BF16)

    def reduction(r, src, from_sib, s0, from_a, s1, from_bz, fin):
        state = {}

        def to_sib():
            state["sib"] = [send(lambda: src.at[:, rows((1 - c) * 16 * r, 16 * r)], from_sib, sib)]

        def to_a():
            for copy in state["sib"]:
                copy.wait_recv()
            for dp in range(2):
                own = src[dp, rows(c * 16 * r, 16 * r), :].astype(F32)
                s0[dp] = (own + from_sib[dp].astype(F32)).astype(BF16)
            state["a"] = [
                send(lambda to=to: s0.at[:, rows(to * 4 * r, 4 * r)], lambda i=i: from_a.at[i], device)
                for i, (to, device) in enumerate(along_a)
            ]

        def to_bz():
            for copy in state["a"]:
                copy.wait_recv()
            for dp in range(2):
                summed = s0[dp, rows(a * 4 * r, 4 * r), :].astype(F32)
                for i in range(3):
                    summed = summed + from_a[i, dp].astype(F32)
                s1[dp] = summed.astype(BF16)
            state["b"] = [
                send(lambda to=to: s1.at[d, rows(to * r, r)], lambda i=i: from_bz.at[i], device)
                for i, (to, device) in enumerate(along_b)
            ]
            for i, (to, device) in enumerate(zip((b, b_up, b_far, b_down), other_plane)):
                state["b"].append(
                    send(lambda to=to: s1.at[d_other, rows(to * r, r)], lambda i=i: from_bz.at[3 + i], device)
                )

        def back_b():
            for copy in state["b"]:
                copy.wait_recv()
            summed = s1[d, rows(b * r, r), :].astype(F32)
            for i in range(7):
                summed = summed + from_bz[i].astype(F32)
            fin[rows(((c * 4 + a) * 4 + b) * r, r), :] = summed.astype(BF16)

            def place():
                return fin.at[rows(((c * 4 + a) * 4 + b) * r, r)]

            state["back_b"] = [send(place, place, device) for _, device in along_b]

        def back_a():
            for copy in state["back_b"]:
                copy.wait_recv()

            def place():
                return fin.at[rows((c * 4 + a) * 4 * r, 4 * r)]

            state["back_a"] = [send(place, place, device) for _, device in along_a]
            state["share"] = [send(place, place, sib)]

        def share():
            for copy, came in zip(state["back_a"], (a_down, a_far, a_up)):
                copy.wait_recv()

                def place(came=came):
                    return fin.at[rows((c * 4 + came) * 4 * r, 4 * r)]

                state["share"].append(send(place, place, sib))

        def end():
            for copy in state["share"]:
                copy.wait_recv()

        return to_sib, to_a, to_bz, back_b, back_a, share, end

    def direct_reduction(r, src, from_sib, s0, from_all, fin, extra):
        state = {}

        def to_sib():
            state["sib"] = [send(lambda: src.at[:, rows((1 - c) * 16 * r, 16 * r)], from_sib, sib)]
            if extra is not None:
                for i, device in enumerate((z_tensor, tensor_sib)):
                    state["sib"].append(
                        send(lambda: src.at[:, pl.ds(NORM_ROWS, 16)], lambda i=i: extra.at[i], device)
                    )

        def to_owner():
            for copy in state["sib"]:
                copy.wait_recv()
            for dp in range(2):
                own = src[dp, rows(c * 16 * r, 16 * r), :].astype(F32)
                s0[dp] = (own + from_sib[dp].astype(F32)).astype(BF16)
            if extra is not None:
                at = NORM_ROWS - 16 * r
                line = lax.broadcasted_iota(jnp.int32, (16, 128), 0)
                mine = (line >= 2) & (line < 6) & (c == 1)
                for dp in range(2):
                    own = src[dp, rows(c * 16 * r + at, 16), :].astype(F32)
                    own = own + from_sib[dp, pl.ds(at, 16), :].astype(F32)
                    more = extra[0, dp].astype(F32) + extra[1, dp].astype(F32)
                    s0[dp, pl.ds(at, 16), :] = (own + jnp.where(mine, more, 0.0)).astype(BF16)
            state["owner"] = send_all(
                [
                    (
                        lambda plane=plane, place=place: s0.at[(d, d_other)[plane], rows((place[0] * 4 + place[1]) * r, r)],
                        lambda i=i: from_all.at[i],
                        device,
                    )
                    for i, plane, place, device in everywhere
                ],
                lambda: from_all.at[pl.ds(1, 31)],
            )

        def back():
            state["owner"].wait_recv()
            summed = s0[d, rows((a * 4 + b) * r, r), :].astype(F32)
            for i in range(1, 32):
                summed = summed + from_all[i].astype(F32)
            fin[rows((c * 16 + a * 4 + b) * r, r), :] = summed.astype(BF16)

            def place():
                return fin.at[rows((c * 16 + a * 4 + b) * r, r)]

            state["back"] = send_all(
                [(place, place, device) for _, plane, _, device in everywhere if plane == 0],
                lambda: from_all.at[pl.ds(1, 15)],
            )

        def share():
            state["back"].wait_recv()

            def place():
                return fin.at[rows(c * 16 * r, 16 * r)]

            state["share"] = send(place, place, sib)

        def end():
            state["share"].wait_recv()

        return to_sib, to_owner, back, share, end

    r1 = reduction(UNITS_1, src1, sib1, s01, ar1, s11, br1, fin1)
    r2 = direct_reduction(UNITS_2, src2, sib2, s02, all2, fin2, tr2)
    r3 = direct_reduction(UNITS_3, src3, sib3, s03, all3, fin3, None)

    acck[...] = jnp.zeros(acck.shape, F32)
    accv[...] = jnp.zeros(accv.shape, F32)

    def backward_start(j):
        at = xs[j] if isinstance(j, int) else (chip_x + 3 * (j == 1).astype(jnp.int32) + (j == 2).astype(jnp.int32)) % 4
        grad = dob[at]
        for h in range(3):
            here = head_lanes(h)
            for first in (HALF, HALF + 16):
                here = here | ((lane >= first + 3 * h) & (lane < first + 3 * h + 3))
            dobig[pl.ds(h * PAD, PAD), :] = jnp.where(here, grad.astype(F32), 0.0).astype(BF16)
        select = lanes_of((16, 256))
        select = jnp.where((select >= HALF + 16) & (select < HALF + 25), 1.0, 0.0).astype(BF16)
        lse_row = mm_nt(select, dobig[...])[0:1, :]
        factor[...] = jnp.exp(mrow[j] - lse_row)

    def backward_half(j, half):
        part_h = pl.ds(half * GROUP, GROUP)
        probs = pt[j, part_h, :].astype(F32) * factor[...]
        grad_scores = (probs * mm_nt(vbuf[part_h, :], dobig[...])).astype(BF16)
        gscore[part_h, :] = grad_scores
        accv[part_h, :] += mm(probs.astype(BF16), dobig[...])
        acck[part_h, :] += mm(grad_scores, qbig[j])

    def backward_end(j):
        grad_q = times([kt[i, 0:HALF, :] for i in range(2)], gscore[...])
        grad_q = jnp.concatenate([own_head(grad_q), jnp.zeros((64, STACK), F32)], axis=0)
        dqm[j] = (mm_nt(picker[...], grad_q.astype(BF16)) * 0.125).astype(BF16)

    grad_parts = {}

    def send_grad(j):
        grad_parts[j] = send(lambda: dqm.at[j], lambda: dqr.at[j - 1], x_dev[j])

    @pl.loop(0, 3)
    def _(j):
        backward_start(j)
        backward_half(j, 1)
        backward_half(j, 0)
        backward_end(j)

        @pl.when(j == 0)
        def _():
            do_near()
            put_wide(src1, 0, mm_tn(grad_low, act[t]))
            put_wide(src1, 1152, mm_tn(n2[...], gup[t]))
            put_rows(src1, 2304, [halves(column_sum(gup[t].astype(F32))), halves(column_sum(gout[...]))])
            src1[:, pl.ds(2320, 240), :] = jnp.zeros((2, 240, 128), BF16)
            r1[0]()

        @pl.when(j == 1)
        def _():
            send_grad(1)

        @pl.when(j == 2)
        def _():
            send_grad(2)
            do_last()

    backward_start(3)
    backward_half(3, 1)
    both_grads = jnp.concatenate([acck[pl.ds(GROUP, GROUP), 0:HALF], accv[pl.ds(GROUP, GROUP), 0:HALF]], axis=1)
    gsib[...] = both_grads.astype(BF16).reshape(4, PAD, WIDE)
    sib_grads = send(gsib, gsibr, sib)
    backward_half(3, 0)
    backward_end(3)
    send_grad(3)
    mixed = mm_nt(act[0], wdt[0]) + mm_nt(act[1], wdt[1])
    yout[...] = (hid[...] + mixed + vfull[5:6, :])[0:OWN].astype(BF16)
    stores = [load(yout, y_ref)]
    both_grads = jnp.concatenate([acck[pl.ds(0, GROUP), 0:HALF], accv[pl.ds(0, GROUP), 0:HALF]], axis=1)
    r1[1]()
    sib_grads.wait_recv()
    gown[...] = both_grads.reshape(4, PAD, WIDE) + gsibr[...].astype(F32)
    gy[...] = gown[...].astype(BF16)
    y_grads = [send(lambda j=j: gy.at[ys[j]], lambda j=j: gyr.at[j - 1], y_dev[j]) for j in (3, 2, 1)]
    attended_low = attx[t]
    for dp in range(2):
        put_tiles(src3, dp, 0, mm_tn(attended_low, grad_h_low[:, dp * HALF : (dp + 1) * HALF]))
    put_rows(
        src3,
        288,
        [halves(column_sum(grad_h)), halves(column_sum(grad_n2 * xhat2)), halves(column_sum(grad_n2))],
    )
    src3[:, pl.ds(304, 208), :] = jnp.zeros((2, 208, 128), BF16)
    r3[0]()
    src2[:, pl.ds(880, 144), :] = jnp.zeros((2, 144, 128), BF16)
    for j in (1, 2, 3):
        grad_parts[j].wait_recv()
    grad_q = dqm[0].astype(F32) + dqr[0].astype(F32) + dqr[1].astype(F32) + dqr[2].astype(F32)
    grad_q = grad_q.astype(BF16)[:, 0:HALF]
    whole = mm_tn(n1[...], grad_q)
    for dp in range(2):
        put_tiles(src2, dp, 0, whole[dp * HALF : (dp + 1) * HALF])
    sum_q = column_sum(grad_q.astype(F32))
    gnq[...] = mm_nt(grad_q, wqf[...])
    r1[2]()
    r3[1]()
    for copy in y_grads:
        copy.wait_recv()
    both_grads = gown[chip_y] + gyr[0].astype(F32) + gyr[1].astype(F32) + gyr[2].astype(F32)
    both_grads = both_grads.astype(BF16)
    grad_k, grad_v = both_grads[:, 0:HALF], both_grads[:, HALF:WIDE]
    grad_n1 = gnq[...] + mm_nt(grad_k, wkf[...]) + mm_nt(grad_v, wvf[...])
    gn1x[t] = grad_n1.astype(BF16)
    gn1_copy = send(gn1x.at[t], gn1x.at[t], z_tensor)
    normed1 = n1[...]
    at = 288
    for grad in (grad_k, grad_v):
        whole = mm_tn(normed1, grad)
        for dp in range(2):
            put_tiles(src2, dp, at, whole[dp * HALF : (dp + 1) * HALF])
        at += 288
    put_rows(
        src2,
        NORM_ROWS,
        [
            halves(sum_q),
            halves(column_sum(grad_v.astype(F32))),
            halves(column_sum(grad_n1 * xh1[...])),
            halves(column_sum(grad_n1)),
        ],
    )
    late_mark = len(sent)
    r2[0]()
    r1[3]()
    r3[2]()
    r2[1]()
    r1[4]()
    gn1_copy.wait_recv()
    grad_n1 = gn1x[0].astype(F32) + gn1x[1].astype(F32)
    xhat1 = xh1[...]
    z = grad_n1 * vfull[0:1, :]
    mean_z = jnp.mean(z, axis=1, keepdims=True)
    mean_zx = jnp.mean(z * xhat1, axis=1, keepdims=True)
    gxout[...] = (ghid[...] + (z - mean_z - xhat1 * mean_zx) * rstd1[...])[0:OWN]
    stores.append(load(gxout, gx_ref))
    r3[3]()
    r2[2]()
    r1[5]()
    r3[4]()
    stores.append(load(fin3, f3_ref))
    flush(late_mark)
    r2[3]()
    r1[6]()
    stores.append(load(fin1, f1_ref))
    r2[4]()
    stores.append(load(fin2, f2_ref))
    flush(len(sent))
    for copy in stores:
        copy.wait()


def finish_kernel(y_ref, gx_ref, f1_hbm, f2_hbm, f3_hbm, *refs):
    outs, refs = refs[:17], refs[17:]
    (f1_ref, f2_ref, f3_ref, gx_in, y_in), kept, (in_sems, out_sems) = refs[:5], refs[5:20], refs[20:]
    o_g1, o_s1, o_wq, o_bq, o_wk, o_wv, o_bv, o_wo, o_bo, o_g2, o_s2, o_wu, o_bu, o_wd, o_bd = kept
    copies = [
        pltpu.make_async_copy(source, target, in_sems.at[i])
        for i, (source, target) in enumerate(
            ((f1_hbm, f1_ref), (f2_hbm, f2_ref), (gx_ref, gx_in.at[0]), (y_ref, y_in.at[0]), (f3_hbm, f3_ref))
        )
    ]
    for copy in copies:
        copy.start()
    stored = []

    def store(*values):
        for value in values:
            i = len(stored)
            target = outs[i_of[id(value)]]
            stored.append(pltpu.make_async_copy(value, target, out_sems.at[i]))
            stored[-1].start()

    i_of = {id(ref): i + 2 for i, ref in enumerate(kept)}
    i_of.update({id(y_in): 0, id(gx_in): 1})

    def take_tiles(ref, at, out):
        r = out.shape[0]
        out[:, 0:128] = ref[pl.ds(at, r), :].astype(F32)
        tail = ref[pl.ds(at + r, r // 2), :].astype(F32)
        out[pl.ds(0, r // 2), 128:HALF] = tail[:, 0:64]
        out[pl.ds(r // 2, r // 2), 128:HALF] = tail[:, 64:128]
        store(out)

    def take_rows(ref, at, outs):
        block = ref[pl.ds(at, 16), :].astype(F32)
        i = 0
        for out in outs:
            size = out.shape[0]
            for j in range(0, size, 128):
                width = min(128, size - j)
                out[pl.ds(j, width)] = jnp.reshape(block[i : i + 1, 0:width], (width,))
                i += 1
            store(out)

    copies[0].wait()
    for at, out in ((0, o_wd), (1152, o_wu)):
        for i in range(6):
            out[:, i * 128 : (i + 1) * 128] = f1_ref[pl.ds(at + i * HALF, HALF), :].astype(F32)
        store(out)
    copies[2].wait()
    store(gx_in)
    copies[3].wait()
    store(y_in)
    take_rows(f1_ref, 2304, [o_bu, o_bd])
    copies[4].wait()
    take_tiles(f3_ref, 0, o_wo)
    take_rows(f3_ref, 288, [o_bo, o_g2, o_s2])
    copies[1].wait()
    take_tiles(f2_ref, 0, o_wq)
    take_tiles(f2_ref, 288, o_wk)
    take_tiles(f2_ref, 576, o_wv)
    take_rows(f2_ref, NORM_ROWS, [o_bq, o_bv, o_g1, o_s1])
    for copy in stored:
        copy.wait()


def vm(*shape, dtype=F32):
    return pltpu.VMEM(shape, dtype)


def reduction_scratch(r, direct):
    steps = [vm(32, r, 128, dtype=BF16)] if direct else [
        vm(3, 2, 4 * r, 128, dtype=BF16),
        vm(2, 4 * r, 128, dtype=BF16),
        vm(7, r, 128, dtype=BF16),
    ]
    return [
        vm(2, 32 * r, 128, dtype=BF16),
        vm(2, 16 * r, 128, dtype=BF16),
        vm(2, 16 * r, 128, dtype=BF16),
        *steps,
        vm(32 * r, 128, dtype=BF16),
    ]


def on_device(*args):
    in_hbm = pl.BlockSpec(memory_space=pltpu.HBM)
    scratch = [
        pltpu.SemaphoreType.DMA((COPIES,)),
        pltpu.SemaphoreType.DMA((COPIES,)),
        pltpu.SemaphoreType.DMA((24,)),
        vm(WIDE, HALF, dtype=BF16),
        vm(WIDE, HALF, dtype=BF16),
        vm(WIDE, HALF, dtype=BF16),
        vm(2, 2, HALF, HALF, dtype=BF16),
        vm(2, WIDE, HID, dtype=BF16),
        vm(2, WIDE, HID, dtype=BF16),
        vm(2, HALF, WIDE, dtype=BF16),
        vm(2, 2, 16, WIDE),
        vm(16, WIDE),
        vm(1, OWN, WIDE, dtype=BF16),
        vm(1, OWN, WIDE, dtype=BF16),
        *[vm(size, dtype=BF16) for size in SMALL],
        vm(2, 4, PAD, WIDE, dtype=BF16),
        vm(4, PAD, WIDE, dtype=BF16),
        vm(2, 4, PAD, WIDE, dtype=BF16),
        vm(4, PAD, WIDE, dtype=BF16),
        vm(4, PAD, 256, dtype=BF16),
        vm(PAD, STACK, dtype=BF16),
        vm(3, WIDE, 256, dtype=BF16),
        vm(2, 256, WIDE, dtype=BF16),
        vm(4, PAD, 256, dtype=BF16),
        vm(4, STACK, 256, dtype=BF16),
        vm(2 * GROUP, 256, dtype=BF16),
        vm(2 * GROUP, 256, dtype=BF16),
        vm(2, 256, GROUP, dtype=BF16),
        vm(2, 256, GROUP, dtype=BF16),
        vm(2, GROUP, 1),
        vm(4, 2 * GROUP, STACK, dtype=BF16),
        vm(4, 1, STACK),
        vm(4, PAD, 256, dtype=BF16),
        vm(3, PAD, 256, dtype=BF16),
        vm(STACK, 256, dtype=BF16),
        vm(1, STACK),
        vm(2 * GROUP, STACK, dtype=BF16),
        vm(2 * GROUP, 256),
        vm(2 * GROUP, 256),
        vm(4, PAD, 256, dtype=BF16),
        vm(3, PAD, 256, dtype=BF16),
        vm(4, PAD, WIDE, dtype=BF16),
        vm(4, PAD, WIDE, dtype=BF16),
        vm(4, PAD, WIDE),
        vm(4, PAD, WIDE, dtype=BF16),
        vm(3, PAD, WIDE, dtype=BF16),
        vm(PAD, WIDE),
        vm(PAD, 1),
        vm(PAD, WIDE, dtype=BF16),
        vm(PAD, WIDE),
        vm(PAD, 256),
        vm(2, PAD, HALF, dtype=BF16),
        vm(PAD, WIDE),
        vm(PAD, WIDE),
        vm(PAD, 1),
        vm(PAD, WIDE, dtype=BF16),
        vm(2, PAD, HID, dtype=BF16),
        vm(2, PAD, HID, dtype=BF16),
        vm(2, PAD, WIDE),
        vm(2, PAD, WIDE, dtype=BF16),
        vm(PAD, WIDE),
        vm(PAD, WIDE),
        *reduction_scratch(UNITS_1, False),
        *reduction_scratch(UNITS_2, True),
        *reduction_scratch(UNITS_3, True),
        vm(2, 2, 16, 128, dtype=BF16),
        vm(OWN, WIDE, dtype=BF16),
        vm(OWN, WIDE),
    ]
    args = list(args)
    args[16] = args[16].T
    specs = [in_hbm] * len(args)
    specs[1] = pl.BlockSpec(memory_space=pltpu.SMEM)
    parts = pl.pallas_call(
        layer_kernel,
        out_shape=[
            jax.ShapeDtypeStruct((OWN, WIDE), BF16),
            jax.ShapeDtypeStruct((OWN, WIDE), F32),
            jax.ShapeDtypeStruct((32 * UNITS_1, 128), BF16),
            jax.ShapeDtypeStruct((32 * UNITS_2, 128), BF16),
            jax.ShapeDtypeStruct((32 * UNITS_3, 128), BF16),
        ],
        in_specs=specs,
        out_specs=[in_hbm] * 5,
        scratch_shapes=scratch,
        compiler_params=pltpu.CompilerParams(
            collective_id=0, has_side_effects=True, vmem_limit_bytes=VMEM_BYTES
        ),
        name="layer",
    )(*args)
    quarter = [
        ((1, OWN, WIDE), BF16), ((1, OWN, WIDE), F32), ((HALF,), F32), ((HALF,), F32), ((HALF, HALF), F32),
        ((96,), F32), ((HALF, HALF), F32), ((HALF, HALF), F32), ((96,), F32), ((HALF, HALF), F32), ((HALF,), F32),
        ((HALF,), F32), ((HALF,), F32), ((HALF, HID), F32), ((WIDE,), F32), ((HALF, HID), F32), ((HALF,), F32),
    ]
    results = list(
        pl.pallas_call(
            finish_kernel,
            out_shape=[jax.ShapeDtypeStruct(shape, dtype) for shape, dtype in quarter],
            in_specs=[in_hbm] * 5,
            out_specs=[in_hbm] * len(quarter),
            scratch_shapes=[
                vm(32 * UNITS_1, 128, dtype=BF16),
                vm(32 * UNITS_2, 128, dtype=BF16),
                vm(32 * UNITS_3, 128, dtype=BF16),
                vm(1, OWN, WIDE),
                vm(1, OWN, WIDE, dtype=BF16),
                *[vm(*shape, dtype=dtype) for shape, dtype in quarter[2:]],
                pltpu.SemaphoreType.DMA((5,)),
                pltpu.SemaphoreType.DMA((17,)),
            ],
            compiler_params=pltpu.CompilerParams(vmem_limit_bytes=VMEM_BYTES),
            name="finish",
        )(*parts)
    )
    results[15] = results[15].T
    return tuple(results)


def solution(mesh):
    wide, split, mixed = P("dp"), P("dp", "tensor"), P(("tensor", "dp"))
    tokens, crossed = P("dp", "ctx", None), P("tensor", "dp")
    return jax.shard_map(
        on_device,
        mesh=mesh,
        in_specs=(
            tokens, P("dp"), tokens, wide, wide, split, mixed, split, split, mixed, crossed, wide,
            wide, wide, split, mixed, crossed, wide,
        ),
        out_specs=(
            tokens, tokens, wide, wide, split, mixed, split, split, mixed, crossed, wide,
            wide, wide, split, mixed, crossed, wide,
        ),
        check_vma=False,
    )
```

time: 579 us -> 86.8 us (0.15)
  waiting for transfers between devices: 326 us -> 0 us
  blocking collectives: 114 us -> 0 us
  Pallas kernels: 0 us -> 85.1 us
  matrix products: 42.9 us -> 0 us
  other arithmetic: 40.3 us -> 0 us
  local copies, waits for them, and re-layouts: 34.2 us -> 0 us
  between operations: 19.5 us -> 1.48 us
    psum x4 -> x0, waiting for transfers between devices: 188 us -> none  [the longest x1 110 us: on_device(): lax.psum(grad_wquery.astype(jnp.bfloat16), 'ctx').astype(jnp.float32)]
    unnamed x14 -> x0, waiting for transfers between devices: 99.9 us -> none
    pallas_call x0 -> x2, Pallas kernels: none -> 85.1 us  [the longest x1 82.4 us: on_device(): pl.pallas_call(layer_kernel, out_shape=[jax.ShapeDtypeStruct((OWN, WIDE),...]
    psum x1 -> x0, blocking collectives: 66.1 us -> none  [on_device(): lax.psum(grad_gain1.astype(jnp.bfloat16), 'ctx').astype(jnp.float32)]
    dot_general x24 -> x0, matrix products: 42.9 us -> none  [the longest x18 25.3 us: product(): return jnp.dot(left, right, preferred_element_type=jnp.float32)]
    all_gather x7 -> x0, blocking collectives: 39 us -> none  [the longest x1 9.25 us: on_device(): lax.all_gather(w_down, 'dp', axis=1, tiled=True)]
    all_gather x1 -> x0, waiting for transfers between devices: 24.6 us -> none  [on_device(): lax.all_gather(jnp.concatenate([keys_own, values_own], axis=1), 'ctx', ax...]
    convert_element_type x26 -> x0, other arithmetic: 20.9 us -> none  [the longest x15 14.9 us: on_device(): owned = (lax.psum_scatter(summed[0].astype(jnp.bfloat16), 'dp', scatter_d...]
  transfers between devices with their start and end apart: 12 -> 0, of which waited for: 8 -> 0; matrix products, arithmetic and copies ran while one was open for 8% -> 0% of each run, Pallas kernels for 0% -> 0%
where the time goes in v1:
time: 86.8 us; the launch traced here: 86.6 us
  Pallas kernels  85.1 us (98%)
  between operations  1.48 us (2%)
    pallas_call x1, Pallas kernels, on_device(): pl.pallas_call(layer_kernel, out_shape=[jax.ShapeDtypeStruct((OWN, WIDE),...  82.4 us
    pallas_call x1, Pallas kernels, on_device(): pl.pallas_call(finish_kernel, out_shape=[jax.ShapeDtypeStruct(shape, dtyp...  2.72 us

profile of v1, /device:TPU:1, one launch (start us, length us, event | category | flops | bytes accessed | tf_op | source)
XLA Modules:
  0.0 86.6 jit_solution(7932369953970192953)
XLA Ops:
  1.3 82.4 %layer.1 = (bf16[136,384]{1,0:T(8,128)(2,1)}, f32[136,384]{1,0:T(8,128)}, bf16[2560,128]{1,0:T(8,128)(2,1)}, bf16[1024,128]{1,0:T(8,128)(2,1)}, bf16[512,128]{1,0:T(8,128)(2,1)}) custom-call(bf16[1,136,384]{2,1,0:T(8,128)(2,1)} %x_ref.1, s32[1]{0:T(128)S(6)} %copy.35.count_ref, bf16[1,136,384]{2,1,0:T(8,128)(2,1)} %cot_ref.1, bf16[192]{0:T(256)(128)(2,1)} %g1_ref.1, ...), custom_call_target="tpu_custom_call" | custom-call | tf_op jit(solution)/shard_map/layer/pallas_call | solution.py:993
  83.7 2.7 %finish.1 = (bf16[1,136,384]{2,1,0:T(8,128)(2,1)}, f32[1,136,384]{2,1,0:T(8,128)}, f32[192]{0:T(256)}, f32[192]{0:T(256)}, f32[192,192]{1,0:T(8,128)}, /*index=5...) custom-call(bf16[136,384]{1,0:T(8,128)(2,1)} %get-tuple-element.39.y, ...), custom_call_target="tpu_custom_call" | custom-call | tf_op jit(solution)/shard_map/finish/pallas_call | solution.py:1016

commit v2 on v1

--- a/solution.py
+++ b/solution.py
@@ -397,24 +397,16 @@
     def send_partial(j):
         partial[j] = send(lambda: om.at[j], lambda: omr.at[j - 1], x_dev[j])
 
-    @pl.loop(0, 4)
-    def _(i):
-        forward(3 - i)
-
-        @pl.when(i == 0)
-        def _():
-            send_partial(3)
-            hand_out()
-            relay("up")
-
-        @pl.when(i == 1)
-        def _():
-            send_partial(2)
-            relay("down")
-
-        @pl.when(i == 2)
-        def _():
-            send_partial(1)
+    forward(3)
+    send_partial(3)
+    hand_out()
+    relay("up")
+    forward(2)
+    send_partial(2)
+    relay("down")
+    forward(1)
+    send_partial(1)
+    forward(0)
 
     x_mark = len(sent)
     for j in (3, 2, 1):
@@ -711,31 +703,24 @@
     def send_grad(j):
         grad_parts[j] = send(lambda: dqm.at[j], lambda: dqr.at[j - 1], x_dev[j])
 
-    @pl.loop(0, 3)
-    def _(j):
+    def backward(j):
         backward_start(j)
         backward_half(j, 1)
         backward_half(j, 0)
         backward_end(j)
 
-        @pl.when(j == 0)
-        def _():
-            do_near()
-            put_wide(src1, 0, mm_tn(grad_low, act[t]))
-            put_wide(src1, 1152, mm_tn(n2[...], gup[t]))
-            put_rows(src1, 2304, [halves(column_sum(gup[t].astype(F32))), halves(column_sum(gout[...]))])
-            src1[:, pl.ds(2320, 240), :] = jnp.zeros((2, 240, 128), BF16)
-            r1[0]()
-
-        @pl.when(j == 1)
-        def _():
-            send_grad(1)
-
-        @pl.when(j == 2)
-        def _():
-            send_grad(2)
-            do_last()
-
+    backward(0)
+    do_near()
+    put_wide(src1, 0, mm_tn(grad_low, act[t]))
+    put_wide(src1, 1152, mm_tn(n2[...], gup[t]))
+    put_rows(src1, 2304, [halves(column_sum(gup[t].astype(F32))), halves(column_sum(gout[...]))])
+    src1[:, pl.ds(2320, 240), :] = jnp.zeros((2, 240, 128), BF16)
+    r1[0]()
+    backward(1)
+    send_grad(1)
+    backward(2)
+    send_grad(2)
+    do_last()
     backward_start(3)
     backward_half(3, 1)
     both_grads = jnp.concatenate([acck[pl.ds(GROUP, GROUP), 0:HALF], accv[pl.ds(GROUP, GROUP), 0:HALF]], axis=1)

time: 86.8 us -> 86.3 us (level)
  no operation moved by 1% of the time
where the time goes in v2:
time: 86.3 us; the launch traced here: 86.1 us
  Pallas kernels  84.6 us (98%)
  between operations  1.48 us (2%)
    pallas_call x1, Pallas kernels, on_device(): pl.pallas_call(layer_kernel, out_shape=[jax.ShapeDtypeStruct((OWN, WIDE),...  81.9 us
    pallas_call x1, Pallas kernels, on_device(): pl.pallas_call(finish_kernel, out_shape=[jax.ShapeDtypeStruct(shape, dtyp...  2.72 us

profile of v2, /device:TPU:1, one launch (start us, length us, event | category | flops | bytes accessed | tf_op | source)
XLA Modules:
  0.0 86.1 jit_solution(3519759054913706394)
XLA Ops:
  1.3 81.9 %layer.1 = (bf16[136,384]{1,0:T(8,128)(2,1)}, f32[136,384]{1,0:T(8,128)}, bf16[2560,128]{1,0:T(8,128)(2,1)}, bf16[1024,128]{1,0:T(8,128)(2,1)}, bf16[512,128]{1,0:T(8,128)(2,1)}) custom-call(bf16[1,136,384]{2,1,0:T(8,128)(2,1)} %x_ref.1, s32[1]{0:T(128)S(6)} %copy.35.count_ref, bf16[1,136,384]{2,1,0:T(8,128)(2,1)} %cot_ref.1, bf16[192]{0:T(256)(128)(2,1)} %g1_ref.1, ...), custom_call_target="tpu_custom_call" | custom-call | tf_op jit(solution)/shard_map/layer/pallas_call | solution.py:978
  83.2 2.7 %finish.1 = (bf16[1,136,384]{2,1,0:T(8,128)(2,1)}, f32[1,136,384]{2,1,0:T(8,128)}, f32[192]{0:T(256)}, f32[192]{0:T(256)}, f32[192,192]{1,0:T(8,128)}, /*index=5...) custom-call(bf16[136,384]{1,0:T(8,128)(2,1)} %get-tuple-element.39.y, ...), custom_call_target="tpu_custom_call" | custom-call | tf_op jit(solution)/shard_map/finish/pallas_call | solution.py:1001
